TPU v7x, 512 devices: a whole 4x4x16 slice. The times are simulated.
512 devices in a mesh: replica: 32 (over z, core), section: 16 (over y, x).
Axes of the slice: x: 4, y: 4, z: 16, core: 2. Of those that a mesh axis runs over, the one named last changes fastest.
Arguments:
- activations: bfloat16 [32, 16, 3, 128, 2688], P('replica', 'section'), may hold values from -64 to 64, as said below
- grad_output: bfloat16 [32, 128, 2688], P('replica'), may hold values from -6 to 6
- gains: float32 [16, 2688], replicated, may hold values from 0.1 to 1.9
- layer_section: int32 [32, 16], P('replica'), may hold values from 0 to 15, as said below
Outputs:
- gain_grad: float32 [16, 2688], P('section', 'replica')
- bias_grad: float32 [16, 2688], P('section', 'replica')
Inputs may be any that keep to these rules, and one draw needn't show every extreme that they name: `layer_section`: each row does not decrease along the layers and starts at 0; its sections are consecutive, each from 0 to the row's largest holds 1 to 3 layers, and the row's largest is at least 9. Some section holds exactly 3 layers and some row uses all 16 sections. `activations`: entries of slots beyond a section's layers are not read.
All inputs are finite; a program needn't handle non-finite values.
Results may differ from a plain program's by a relative error of at most 0.011.
Values may be sent and summed in bfloat16 or wider, within the bound.
No kernel may reach another device: no remote copies, remote signals or barrier semaphores. Data moves between devices by JAX's collectives and lax.ppermute only.
A program may use at most 64 MiB of HBM per device.

v0:
```python
import jax
import jax.numpy as jnp
from jax import lax
from jax.sharding import PartitionSpec as P

epsilon = 1e-05


def passed_along(block, axis, distance):
    devices = range(lax.axis_size(axis))
    route = [(i - distance, i) for i in devices if i - distance in devices]
    return lax.ppermute(block, axis, route)


def layer_backward(gradient, saved_rows, gain_row):
    values = saved_rows.astype(jnp.float32)
    average = jnp.mean(values, axis=-1, keepdims=True)
    centered = values - average
    variance = jnp.mean(centered * centered, axis=-1, keepdims=True)
    inverse = lax.rsqrt(variance + epsilon)
    normed = centered * inverse
    incoming = gradient.astype(jnp.float32)
    scaled = gain_row[None, :] * incoming
    update = (
        scaled
        - jnp.mean(scaled, axis=-1, keepdims=True)
        - normed * jnp.mean(scaled * normed, axis=-1, keepdims=True)
    )
    outgoing = (incoming + inverse * update).astype(jnp.bfloat16)
    partial_value = jnp.stack([jnp.sum(incoming * normed, axis=0), jnp.sum(incoming, axis=0)])
    return (outgoing, partial_value)


def section_backward(gradient, saved_block, gains, first_layer, layer_count):
    slot_count = saved_block.shape[0]
    channels = saved_block.shape[2]
    partials = [None] * slot_count
    for slot_index in reversed(range(slot_count)):
        active = slot_index < layer_count
        layer_index = jnp.clip(first_layer + slot_index, 0, gains.shape[0] - 1)
        gain_row = lax.dynamic_index_in_dim(gains, layer_index, 0, keepdims=False)
        saved_rows = saved_block[slot_index]

        def compute_slot(current, rows=saved_rows, row_gain=gain_row):
            return layer_backward(current, rows, row_gain)

        def skip_slot(current):
            return (current, jnp.zeros((2, channels), jnp.float32))

        gradient, partial_value = lax.cond(active, compute_slot, skip_slot, gradient)
        partials[slot_index] = partial_value
    return (gradient, jnp.stack(partials))


def local(activations, grad_output, gains, layer_section):
    saved_inputs = activations[0, 0]
    start_grad = grad_output[0]
    section_map = layer_section[0]
    layers = gains.shape[0]
    slot_count = saved_inputs.shape[0]
    tokens = saved_inputs.shape[1]
    channels = saved_inputs.shape[2]
    sections = lax.axis_size("section")
    replicas = lax.axis_size("replica")
    position = lax.axis_index("section")
    layer_count = jnp.sum((section_map == position).astype(jnp.int32))
    first_layer = jnp.sum((section_map < position).astype(jnp.int32))
    group_count = 1
    block_rows = tokens // group_count

    def run_turn(turn_index, carried):
        buffer, partials = carried
        token_group = turn_index - (sections - 1 - position)
        active_turn = (token_group >= 0) & (token_group < group_count)
        incoming = jnp.where(position == sections - 1, start_grad, buffer)

        def do_layers():
            outgoing, fresh = section_backward(
                incoming, saved_inputs, gains, first_layer, layer_count
            )
            return (outgoing, partials + fresh)

        def pass_along():
            return (incoming, partials)

        return lax.cond(active_turn, do_layers, pass_along)

    def advance(turn_index, carried):
        buffer, partials = run_turn(turn_index, carried)
        return (passed_along(buffer, "section", -1), partials)

    initial = (
        jnp.zeros((block_rows, channels), jnp.bfloat16),
        jnp.zeros((slot_count, 2, channels), jnp.float32),
    )
    carried = lax.fori_loop(0, sections + group_count - 2, advance, initial)
    unused, partials = run_turn(sections + group_count - 2, carried)
    slot_ids = jnp.arange(slot_count)
    row_layers = layers - 1 - jnp.arange(layers)
    owner_table = (
        ((first_layer + slot_ids)[:, None] == row_layers[None, :])
        & (slot_ids < layer_count)[:, None]
    ).astype(jnp.float32)
    grad_table = jnp.einsum("jl,jcd->cld", owner_table, partials, precision=lax.Precision.HIGHEST)
    layers_each = layers // sections
    column_count = channels // replicas
    summed = lax.psum(grad_table, ("replica", "section"))
    owned = lax.dynamic_slice(
        summed,
        (0, position * layers_each, lax.axis_index("replica") * column_count),
        (2, layers_each, column_count),
    )
    owned = owned / replicas
    return (owned[0], owned[1])


def solution(mesh):
    placed = (
        P("replica", "section", None, None, None),
        P("replica", None, None),
        P(),
        P("replica", None),
    )
    return jax.shard_map(
        local,
        mesh=mesh,
        in_specs=placed,
        out_specs=(P("section", "replica"), P("section", "replica")),
        check_vma=False,
    )
```

profile of v0, /device:TPU:1, one launch (start us, length us, event | category | flops | bytes accessed | tf_op | source)
XLA Modules:
  0.0 835.7 jit_solution(3795330015678609533)
XLA Ops:
  7.2 1.4 fusion.77
  10.0 320.0 %while.20 = (s32[]{:T(128)}, bf16[128,2688]{1,0:T(8,128)(2,1)S(1)}, f32[3,2,2688]{2,1,0:T(2,128)S(1)}, s32[]{:T(128)}, pred[]{:T(512)}, /*index=5*/bf16[128,2688...) while((s32[]{:T(128)}, bf16[128,2688]{1,0:T(8,128)(2,1)S(1)}, ...), condition=%wide.region_29.30_spmd, body=%wide.region_2.29_spmd.sunk | while | flops 29294228 | bytes 28200028 | solution.py:96
  10.1 1.4 copy-done
  11.6 1.3 collective-permute-start
  12.9 11.8 %collective-permute-done = bf16[128,2688]{1,0:T(8,128)(2,1)S(1)} collective-permute-done((bf16[128,2688]{1,0:T(8,128)(2,1)S(1)}, bf16[128,2688]{1,0:T(8,128)(2,1)S(1)}, u32[]{:S(2)}, u32[]{:S(2)}) %collective-permute-start) | collective-permute-done | bytes 688160 | tf_op jit(solution)/shard_map/while/body/eval_jaxpr/ppermute | solution.py:12
  24.8 1.5 copy-done
  26.2 1.3 collective-permute-start
  27.5 21.6 %collective-permute-done = bf16[128,2688]{1,0:T(8,128)(2,1)S(1)} collective-permute-done((bf16[128,2688]{1,0:T(8,128)(2,1)S(1)}, bf16[128,2688]{1,0:T(8,128)(2,1)S(1)}, u32[]{:S(2)}, u32[]{:S(2)}) %collective-permute-start) | collective-permute-done | bytes 688160 | tf_op jit(solution)/shard_map/while/body/eval_jaxpr/ppermute | solution.py:12
  49.3 1.5 copy-done
  50.8 1.3 collective-permute-start
  52.1 15.1 %collective-permute-done = bf16[128,2688]{1,0:T(8,128)(2,1)S(1)} collective-permute-done((bf16[128,2688]{1,0:T(8,128)(2,1)S(1)}, bf16[128,2688]{1,0:T(8,128)(2,1)S(1)}, u32[]{:S(2)}, u32[]{:S(2)}) %collective-permute-start) | collective-permute-done | bytes 688160 | tf_op jit(solution)/shard_map/while/body/eval_jaxpr/ppermute | solution.py:12
  67.2 1.5 copy-done
  68.7 1.3 collective-permute-start
  70.0 17.1 %collective-permute-done = bf16[128,2688]{1,0:T(8,128)(2,1)S(1)} collective-permute-done((bf16[128,2688]{1,0:T(8,128)(2,1)S(1)}, bf16[128,2688]{1,0:T(8,128)(2,1)S(1)}, u32[]{:S(2)}, u32[]{:S(2)}) %collective-permute-start) | collective-permute-done | bytes 688160 | tf_op jit(solution)/shard_map/while/body/eval_jaxpr/ppermute | solution.py:12
  87.2 1.5 copy-done
  88.7 1.3 collective-permute-start
  90.0 15.3 %collective-permute-done = bf16[128,2688]{1,0:T(8,128)(2,1)S(1)} collective-permute-done((bf16[128,2688]{1,0:T(8,128)(2,1)S(1)}, bf16[128,2688]{1,0:T(8,128)(2,1)S(1)}, u32[]{:S(2)}, u32[]{:S(2)}) %collective-permute-start) | collective-permute-done | bytes 688160 | tf_op jit(solution)/shard_map/while/body/eval_jaxpr/ppermute | solution.py:12
  105.4 1.5 copy-done
  106.9 1.3 collective-permute-start
  108.2 14.4 %collective-permute-done = bf16[128,2688]{1,0:T(8,128)(2,1)S(1)} collective-permute-done((bf16[128,2688]{1,0:T(8,128)(2,1)S(1)}, bf16[128,2688]{1,0:T(8,128)(2,1)S(1)}, u32[]{:S(2)}, u32[]{:S(2)}) %collective-permute-start) | collective-permute-done | bytes 688160 | tf_op jit(solution)/shard_map/while/body/eval_jaxpr/ppermute | solution.py:12
  122.7 1.5 copy-done
  124.2 1.3 collective-permute-start
  125.4 13.5 %collective-permute-done = bf16[128,2688]{1,0:T(8,128)(2,1)S(1)} collective-permute-done((bf16[128,2688]{1,0:T(8,128)(2,1)S(1)}, bf16[128,2688]{1,0:T(8,128)(2,1)S(1)}, u32[]{:S(2)}, u32[]{:S(2)}) %collective-permute-start) | collective-permute-done | bytes 688160 | tf_op jit(solution)/shard_map/while/body/eval_jaxpr/ppermute | solution.py:12
  139.0 1.5 copy-done
  140.5 1.3 collective-permute-start
  141.8 12.6 %collective-permute-done = bf16[128,2688]{1,0:T(8,128)(2,1)S(1)} collective-permute-done((bf16[128,2688]{1,0:T(8,128)(2,1)S(1)}, bf16[128,2688]{1,0:T(8,128)(2,1)S(1)}, u32[]{:S(2)}, u32[]{:S(2)}) %collective-permute-start) | collective-permute-done | bytes 688160 | tf_op jit(solution)/shard_map/while/body/eval_jaxpr/ppermute | solution.py:12
  154.5 1.5 copy-done
  155.9 1.3 collective-permute-start
  157.2 11.6 %collective-permute-done = bf16[128,2688]{1,0:T(8,128)(2,1)S(1)} collective-permute-done((bf16[128,2688]{1,0:T(8,128)(2,1)S(1)}, bf16[128,2688]{1,0:T(8,128)(2,1)S(1)}, u32[]{:S(2)}, u32[]{:S(2)}) %collective-permute-start) | collective-permute-done | bytes 688160 | tf_op jit(solution)/shard_map/while/body/eval_jaxpr/ppermute | solution.py:12
  169.0 1.5 copy-done
  170.4 1.3 collective-permute-start
  171.7 12.1 %collective-permute-done = bf16[128,2688]{1,0:T(8,128)(2,1)S(1)} collective-permute-done((bf16[128,2688]{1,0:T(8,128)(2,1)S(1)}, bf16[128,2688]{1,0:T(8,128)(2,1)S(1)}, u32[]{:S(2)}, u32[]{:S(2)}) %collective-permute-start) | collective-permute-done | bytes 688160 | tf_op jit(solution)/shard_map/while/body/eval_jaxpr/ppermute | solution.py:12
  184.0 1.5 copy-done
  185.4 1.3 collective-permute-start
  186.7 13.3 %collective-permute-done = bf16[128,2688]{1,0:T(8,128)(2,1)S(1)} collective-permute-done((bf16[128,2688]{1,0:T(8,128)(2,1)S(1)}, bf16[128,2688]{1,0:T(8,128)(2,1)S(1)}, u32[]{:S(2)}, u32[]{:S(2)}) %collective-permute-start) | collective-permute-done | bytes 688160 | tf_op jit(solution)/shard_map/while/body/eval_jaxpr/ppermute | solution.py:12
  200.1 1.5 copy-done
  201.6 1.3 collective-permute-start
  202.9 14.8 %collective-permute-done = bf16[128,2688]{1,0:T(8,128)(2,1)S(1)} collective-permute-done((bf16[128,2688]{1,0:T(8,128)(2,1)S(1)}, bf16[128,2688]{1,0:T(8,128)(2,1)S(1)}, u32[]{:S(2)}, u32[]{:S(2)}) %collective-permute-start) | collective-permute-done | bytes 688160 | tf_op jit(solution)/shard_map/while/body/eval_jaxpr/ppermute | solution.py:12
  217.8 1.5 copy-done
  219.3 1.3 collective-permute-start
  220.6 16.4 %collective-permute-done = bf16[128,2688]{1,0:T(8,128)(2,1)S(1)} collective-permute-done((bf16[128,2688]{1,0:T(8,128)(2,1)S(1)}, bf16[128,2688]{1,0:T(8,128)(2,1)S(1)}, u32[]{:S(2)}, u32[]{:S(2)}) %collective-permute-start) | collective-permute-done | bytes 688160 | tf_op jit(solution)/shard_map/while/body/eval_jaxpr/ppermute | solution.py:12
  237.1 1.5 copy-done
  238.6 1.3 collective-permute-start
  239.9 17.5 %collective-permute-done = bf16[128,2688]{1,0:T(8,128)(2,1)S(1)} collective-permute-done((bf16[128,2688]{1,0:T(8,128)(2,1)S(1)}, bf16[128,2688]{1,0:T(8,128)(2,1)S(1)}, u32[]{:S(2)}, u32[]{:S(2)}) %collective-permute-start) | collective-permute-done | bytes 688160 | tf_op jit(solution)/shard_map/while/body/eval_jaxpr/ppermute | solution.py:12
  257.5 1.5 copy-done
  260.3 69.7 %collective-permute-done = bf16[128,2688]{1,0:T(8,128)(2,1)S(1)} collective-permute-done((bf16[128,2688]{1,0:T(8,128)(2,1)S(1)}, bf16[128,2688]{1,0:T(8,128)(2,1)S(1)}, u32[]{:S(2)}, u32[]{:S(2)}) %collective-permute-start) | collective-permute-done | bytes 688160 | tf_op jit(solution)/shard_map/while/body/eval_jaxpr/ppermute | solution.py:12
  330.0 4.1 conditional.8
  335.2 492.3 %all-reduce.2.cloned.1.call-done = f32[2,16,2688]{2,1,0:T(8,128)} async-done(((f32[2,16,2688]{2,1,0:T(8,128)}), f32[2,16,2688]{2,1,0:T(8,128)}) %all-reduce.2.cloned.1.call-update) | async-done | bytes 344080 | tf_op jit(solution)/shard_map/psum | solution.py:107
  (74 shorter events, 10.0 us)
Async XLA Ops:
  7.2 820.4 %all-reduce.2.cloned.1.call-start = ((), (), s32[]{:S(2)}) async-start(), calls=%async_computation | async-start | bytes 688128 | tf_op jit(solution)/shard_map/psum | solution.py:107
  10.0 1.6 copy-start
  11.6 13.1 %collective-permute-start = (bf16[128,2688]{1,0:T(8,128)(2,1)S(1)}, bf16[128,2688]{1,0:T(8,128)(2,1)S(1)}, u32[]{:S(2)}, u32[]{:S(2)}) collective-permute-start(bf16[128,2688]{1,0:T(8,128)(2,1)S(1)} %get-tuple-element.613), channel_id=1, source_target_pairs={{1,0},{2,1},{3,2},{4,3},{5,4},{6,5},{7,6},{8,7},{9,8},{10,9},{11,1... | collective-permute-start | bytes 2064392 | tf_op jit(solution)/shard_map/while/body/eval_jaxpr/ppermute | solution.py:12
  24.7 1.6 copy-start
  26.2 22.9 %collective-permute-start = (bf16[128,2688]{1,0:T(8,128)(2,1)S(1)}, bf16[128,2688]{1,0:T(8,128)(2,1)S(1)}, u32[]{:S(2)}, u32[]{:S(2)}) collective-permute-start(bf16[128,2688]{1,0:T(8,128)(2,1)S(1)} %get-tuple-element.613), channel_id=1, source_target_pairs={{1,0},{2,1},{3,2},{4,3},{5,4},{6,5},{7,6},{8,7},{9,8},{10,9},{11,1... | collective-permute-start | bytes 2064392 | tf_op jit(solution)/shard_map/while/body/eval_jaxpr/ppermute | solution.py:12
  49.2 1.6 copy-start
  50.8 16.3 %collective-permute-start = (bf16[128,2688]{1,0:T(8,128)(2,1)S(1)}, bf16[128,2688]{1,0:T(8,128)(2,1)S(1)}, u32[]{:S(2)}, u32[]{:S(2)}) collective-permute-start(bf16[128,2688]{1,0:T(8,128)(2,1)S(1)} %get-tuple-element.613), channel_id=1, source_target_pairs={{1,0},{2,1},{3,2},{4,3},{5,4},{6,5},{7,6},{8,7},{9,8},{10,9},{11,1... | collective-permute-start | bytes 2064392 | tf_op jit(solution)/shard_map/while/body/eval_jaxpr/ppermute | solution.py:12
  67.1 1.6 copy-start
  68.7 18.4 %collective-permute-start = (bf16[128,2688]{1,0:T(8,128)(2,1)S(1)}, bf16[128,2688]{1,0:T(8,128)(2,1)S(1)}, u32[]{:S(2)}, u32[]{:S(2)}) collective-permute-start(bf16[128,2688]{1,0:T(8,128)(2,1)S(1)} %get-tuple-element.613), channel_id=1, source_target_pairs={{1,0},{2,1},{3,2},{4,3},{5,4},{6,5},{7,6},{8,7},{9,8},{10,9},{11,1... | collective-permute-start | bytes 2064392 | tf_op jit(solution)/shard_map/while/body/eval_jaxpr/ppermute | solution.py:12
  87.1 1.6 copy-start
  88.7 16.6 %collective-permute-start = (bf16[128,2688]{1,0:T(8,128)(2,1)S(1)}, bf16[128,2688]{1,0:T(8,128)(2,1)S(1)}, u32[]{:S(2)}, u32[]{:S(2)}) collective-permute-start(bf16[128,2688]{1,0:T(8,128)(2,1)S(1)} %get-tuple-element.613), channel_id=1, source_target_pairs={{1,0},{2,1},{3,2},{4,3},{5,4},{6,5},{7,6},{8,7},{9,8},{10,9},{11,1... | collective-permute-start | bytes 2064392 | tf_op jit(solution)/shard_map/while/body/eval_jaxpr/ppermute | solution.py:12
  105.3 1.6 copy-start
  106.9 15.7 %collective-permute-start = (bf16[128,2688]{1,0:T(8,128)(2,1)S(1)}, bf16[128,2688]{1,0:T(8,128)(2,1)S(1)}, u32[]{:S(2)}, u32[]{:S(2)}) collective-permute-start(bf16[128,2688]{1,0:T(8,128)(2,1)S(1)} %get-tuple-element.613), channel_id=1, source_target_pairs={{1,0},{2,1},{3,2},{4,3},{5,4},{6,5},{7,6},{8,7},{9,8},{10,9},{11,1... | collective-permute-start | bytes 2064392 | tf_op jit(solution)/shard_map/while/body/eval_jaxpr/ppermute | solution.py:12
  122.6 1.6 copy-start
  124.2 14.8 %collective-permute-start = (bf16[128,2688]{1,0:T(8,128)(2,1)S(1)}, bf16[128,2688]{1,0:T(8,128)(2,1)S(1)}, u32[]{:S(2)}, u32[]{:S(2)}) collective-permute-start(bf16[128,2688]{1,0:T(8,128)(2,1)S(1)} %get-tuple-element.613), channel_id=1, source_target_pairs={{1,0},{2,1},{3,2},{4,3},{5,4},{6,5},{7,6},{8,7},{9,8},{10,9},{11,1... | collective-permute-start | bytes 2064392 | tf_op jit(solution)/shard_map/while/body/eval_jaxpr/ppermute | solution.py:12
  138.9 1.6 copy-start
  140.5 13.8 %collective-permute-start = (bf16[128,2688]{1,0:T(8,128)(2,1)S(1)}, bf16[128,2688]{1,0:T(8,128)(2,1)S(1)}, u32[]{:S(2)}, u32[]{:S(2)}) collective-permute-start(bf16[128,2688]{1,0:T(8,128)(2,1)S(1)} %get-tuple-element.613), channel_id=1, source_target_pairs={{1,0},{2,1},{3,2},{4,3},{5,4},{6,5},{7,6},{8,7},{9,8},{10,9},{11,1... | collective-permute-start | bytes 2064392 | tf_op jit(solution)/shard_map/while/body/eval_jaxpr/ppermute | solution.py:12
  154.3 1.6 copy-start
  155.9 12.9 %collective-permute-start = (bf16[128,2688]{1,0:T(8,128)(2,1)S(1)}, bf16[128,2688]{1,0:T(8,128)(2,1)S(1)}, u32[]{:S(2)}, u32[]{:S(2)}) collective-permute-start(bf16[128,2688]{1,0:T(8,128)(2,1)S(1)} %get-tuple-element.613), channel_id=1, source_target_pairs={{1,0},{2,1},{3,2},{4,3},{5,4},{6,5},{7,6},{8,7},{9,8},{10,9},{11,1... | collective-permute-start | bytes 2064392 | tf_op jit(solution)/shard_map/while/body/eval_jaxpr/ppermute | solution.py:12
  168.9 1.6 copy-start
  170.4 13.4 %collective-permute-start = (bf16[128,2688]{1,0:T(8,128)(2,1)S(1)}, bf16[128,2688]{1,0:T(8,128)(2,1)S(1)}, u32[]{:S(2)}, u32[]{:S(2)}) collective-permute-start(bf16[128,2688]{1,0:T(8,128)(2,1)S(1)} %get-tuple-element.613), channel_id=1, source_target_pairs={{1,0},{2,1},{3,2},{4,3},{5,4},{6,5},{7,6},{8,7},{9,8},{10,9},{11,1... | collective-permute-start | bytes 2064392 | tf_op jit(solution)/shard_map/while/body/eval_jaxpr/ppermute | solution.py:12
  183.9 1.6 copy-start
  185.4 14.6 %collective-permute-start = (bf16[128,2688]{1,0:T(8,128)(2,1)S(1)}, bf16[128,2688]{1,0:T(8,128)(2,1)S(1)}, u32[]{:S(2)}, u32[]{:S(2)}) collective-permute-start(bf16[128,2688]{1,0:T(8,128)(2,1)S(1)} %get-tuple-element.613), channel_id=1, source_target_pairs={{1,0},{2,1},{3,2},{4,3},{5,4},{6,5},{7,6},{8,7},{9,8},{10,9},{11,1... | collective-permute-start | bytes 2064392 | tf_op jit(solution)/shard_map/while/body/eval_jaxpr/ppermute | solution.py:12
  200.0 1.6 copy-start
  201.6 16.1 %collective-permute-start = (bf16[128,2688]{1,0:T(8,128)(2,1)S(1)}, bf16[128,2688]{1,0:T(8,128)(2,1)S(1)}, u32[]{:S(2)}, u32[]{:S(2)}) collective-permute-start(bf16[128,2688]{1,0:T(8,128)(2,1)S(1)} %get-tuple-element.613), channel_id=1, source_target_pairs={{1,0},{2,1},{3,2},{4,3},{5,4},{6,5},{7,6},{8,7},{9,8},{10,9},{11,1... | collective-permute-start | bytes 2064392 | tf_op jit(solution)/shard_map/while/body/eval_jaxpr/ppermute | solution.py:12
  217.7 1.6 copy-start
  219.3 17.7 %collective-permute-start = (bf16[128,2688]{1,0:T(8,128)(2,1)S(1)}, bf16[128,2688]{1,0:T(8,128)(2,1)S(1)}, u32[]{:S(2)}, u32[]{:S(2)}) collective-permute-start(bf16[128,2688]{1,0:T(8,128)(2,1)S(1)} %get-tuple-element.613), channel_id=1, source_target_pairs={{1,0},{2,1},{3,2},{4,3},{5,4},{6,5},{7,6},{8,7},{9,8},{10,9},{11,1... | collective-permute-start | bytes 2064392 | tf_op jit(solution)/shard_map/while/body/eval_jaxpr/ppermute | solution.py:12
  237.0 1.6 copy-start
  238.6 18.8 %collective-permute-start = (bf16[128,2688]{1,0:T(8,128)(2,1)S(1)}, bf16[128,2688]{1,0:T(8,128)(2,1)S(1)}, u32[]{:S(2)}, u32[]{:S(2)}) collective-permute-start(bf16[128,2688]{1,0:T(8,128)(2,1)S(1)} %get-tuple-element.613), channel_id=1, source_target_pairs={{1,0},{2,1},{3,2},{4,3},{5,4},{6,5},{7,6},{8,7},{9,8},{10,9},{11,1... | collective-permute-start | bytes 2064392 | tf_op jit(solution)/shard_map/while/body/eval_jaxpr/ppermute | solution.py:12
  257.4 1.6 copy-start
  259.0 71.0 %collective-permute-start = (bf16[128,2688]{1,0:T(8,128)(2,1)S(1)}, bf16[128,2688]{1,0:T(8,128)(2,1)S(1)}, u32[]{:S(2)}, u32[]{:S(2)}) collective-permute-start(bf16[128,2688]{1,0:T(8,128)(2,1)S(1)} %get-tuple-element.613), channel_id=1, source_target_pairs={{1,0},{2,1},{3,2},{4,3},{5,4},{6,5},{7,6},{8,7},{9,8},{10,9},{11,1... | collective-permute-start | bytes 2064392 | tf_op jit(solution)/shard_map/while/body/eval_jaxpr/ppermute | solution.py:12
  330.0 1.6 copy-start.1
Sparse Core Ops, SparseCore 0:
  335.3 492.1 all-reduce.1
where the time goes:
time: 837 us; the launch traced here: 836 us
  waiting for transfers between devices  769 us (92%)
  local copies, waits for them, and re-layouts  23.2 us (3%)
  starting transfers between devices  19.2 us (2%)
  between operations  14.1 us (2%)
    psum x1, waiting for transfers between devices, local(): summed = lax.psum(grad_table, ('replica', 'section'))  492 us
    ppermute x15, waiting for transfers between devices, passed_along(): return lax.ppermute(block, axis, route)  277 us
    while x30, local copies, waits for them, and re-layouts  21.9 us
    ppermute x15, starting transfers between devices, passed_along(): return lax.ppermute(block, axis, route)  19.2 us
  transfers between devices with their start and end apart: 16, of which 16 were waited for; matrix products, arithmetic and copies ran while one was open for 0% of the time, Pallas kernels for 0%

commit v1 on v0

v1 whole, which is shorter than its diff:
```python
import jax
import jax.numpy as jnp
from jax import lax
from jax.experimental import pallas as pl
from jax.experimental.pallas import tpu as pltpu
from jax.sharding import PartitionSpec as P

epsilon = 1e-05
lanes = 128


def total(terms):
    while len(terms) > 1:
        pairs = [left + right for left, right in zip(terms[::2], terms[1::2])]
        terms = pairs + terms[len(terms) - len(terms) % 2:]
    return terms[0]


def across(tile):
    return jnp.broadcast_to(jnp.sum(tile, axis=1, keepdims=True), tile.shape)


def fold(tiles):
    index = lax.broadcasted_iota(jnp.int32, tiles[0].shape, 0)
    low = index < 4
    quads = [
        jnp.where(low, a, b) + pltpu.roll(jnp.where(low, b, a), 4, 0) for a, b in zip(tiles[:4], tiles[4:])
    ]
    low = index % 4 < 2
    pairs = [
        jnp.where(low, a + pltpu.roll(a, 6, 0), b + pltpu.roll(b, 2, 0)) for a, b in zip(quads[:2], quads[2:])
    ]
    a, b = pairs
    return jnp.where(index % 2 < 1, a + pltpu.roll(a, 7, 0), b + pltpu.roll(b, 1, 0))


def relay_kernel(position_ref, map_ref, slots_ref, grad_ref, gains_ref, out_ref, held_ref, normed_ref, sem):
    layers, rows, channels = normed_ref.shape
    slot_count = slots_ref.shape[0] // out_ref.shape[0]
    columns = [slice(at, at + lanes) for at in range(0, channels, lanes)]
    share = 1.0 / channels
    fetch = pltpu.make_async_copy(grad_ref.at[position_ref[0]], held_ref, sem)
    fetch.start()
    places, slot = [], 0
    for layer in range(layers):
        if layer:
            slot = jnp.where(map_ref[layer] == map_ref[layer - 1], slot + 1, 0)
        places.append(map_ref[layer] * slot_count + slot)

    def tiles(layer):
        return [slots_ref[places[layer], :, at].astype(jnp.float32) for at in columns]

    order = list(reversed(range(layers)))
    average = {layer: across(total(tiles(layer))) * share for layer in order}
    inverse = {}
    for layer in order:
        centered = [tile - average[layer] for tile in tiles(layer)]
        inverse[layer] = lax.rsqrt(across(total([tile * tile for tile in centered])) * share + epsilon)
    for layer in order:
        for at, tile in zip(columns, tiles(layer)):
            normed_ref[layer, :, at] = (tile - average[layer]) * inverse[layer]
    fetch.wait()
    gradient = [held_ref[:, at].astype(jnp.float32) for at in columns]
    blank = jnp.zeros((rows, lanes), jnp.float32)
    for layer in order:
        normed = [normed_ref[layer, :, at] for at in columns]
        along = [g * n for g, n in zip(gradient, normed)]
        gain = [gains_ref[layer:layer + 1, at] for at in columns]
        scaled = [g * c for g, c in zip(gradient, gain)]
        along_one = across(total(scaled)) * share * inverse[layer]
        along_normed = across(total([p * c for p, c in zip(along, gain)])) * share * inverse[layer]
        sums = along + gradient
        sums = sums + [blank] * (-len(sums) % 16)
        row = layers - 1 - layer
        for at in range(0, len(sums), 16):
            packed = jnp.concatenate([fold(sums[at:at + 8]), fold(sums[at + 8:at + 16])], axis=0)
            out_ref[row, at:at + 16] = packed.astype(out_ref.dtype)
        gradient = [
            (g + inverse[layer] * u) - (along_one + along_normed * n)
            for g, u, n in zip(gradient, scaled, normed)
        ]


def relay(position, section_map, slots, grad, gains):
    layers, channels = gains.shape
    _, rows, _ = grad.shape
    packed_rows = -(-2 * channels // lanes // 16) * 16
    return pl.pallas_call(
        relay_kernel,
        grid_spec=pltpu.PrefetchScalarGridSpec(
            num_scalar_prefetch=2,
            grid=(),
            in_specs=[
                pl.BlockSpec(memory_space=pltpu.VMEM),
                pl.BlockSpec(memory_space=pl.ANY),
                pl.BlockSpec(memory_space=pltpu.VMEM),
            ],
            out_specs=pl.BlockSpec(memory_space=pltpu.VMEM),
            scratch_shapes=[
                pltpu.VMEM((rows, channels), grad.dtype),
                pltpu.VMEM((layers, rows, channels), jnp.float32),
                pltpu.SemaphoreType.DMA,
            ],
        ),
        out_shape=jax.ShapeDtypeStruct((layers, packed_rows, lanes), jnp.bfloat16),
        compiler_params=pltpu.CompilerParams(vmem_limit_bytes=24 * 1024 * 1024),
        cost_estimate=pl.CostEstimate(
            flops=30 * layers * rows * channels, bytes_accessed=4 * layers * rows * channels, transcendentals=0
        ),
    )(position, section_map, slots, grad, gains)


def summed(block, axis):
    received = lax.all_to_all(block, axis, 0, 0)
    return jnp.sum(received.astype(jnp.float32), axis=0)


def local(activations, grad_output, gains, layer_section):
    saved = activations[0, 0]
    slot_count, tokens, channels = saved.shape
    layers = gains.shape[0]
    sections = lax.axis_size("section")
    replicas = lax.axis_size("replica")
    position = jnp.full((1,), lax.axis_index("section"), jnp.int32)
    rows = tokens // sections
    blocks = saved.reshape(slot_count, sections, rows, channels)
    received = lax.all_to_all(blocks, "section", 1, 0)
    slots = received.reshape(sections * slot_count, rows, channels)
    grad = grad_output[0].reshape(sections, rows, channels)
    partials = relay(position, layer_section[0], slots, grad, gains)
    mine = summed(partials, "section")
    pieces = mine.reshape(-1)[: 2 * channels].reshape(2, replicas, channels // replicas)
    owned = summed(jnp.transpose(pieces, (1, 0, 2)), "replica") / replicas
    return (owned[:1], owned[1:])


def solution(mesh):
    placed = (
        P("replica", "section", None, None, None),
        P("replica", None, None),
        P(),
        P("replica", None),
    )
    return jax.shard_map(
        local,
        mesh=mesh,
        in_specs=placed,
        out_specs=(P("section", "replica"), P("section", "replica")),
        check_vma=False,
    )
```

time: 837 us -> 86 us (0.10)
  waiting for transfers between devices: 769 us -> 24.8 us
  blocking collectives: 0 us -> 46.1 us
  local copies, waits for them, and re-layouts: 23.2 us -> 3.73 us
  between operations: 14.1 us -> 0.67 us
  starting transfers between devices: 19.2 us -> 7.72 us
    psum x1 -> x0, waiting for transfers between devices: 492 us -> none  [local(): summed = lax.psum(grad_table, ('replica', 'section'))]
    ppermute x15 -> x0, waiting for transfers between devices: 277 us -> none  [passed_along(): return lax.ppermute(block, axis, route)]
    all_to_all x0 -> x2, blocking collectives: none -> 46.1 us  [summed(): received = lax.all_to_all(block, axis, 0, 0)]
    all_to_all x0 -> x1, waiting for transfers between devices: none -> 24.8 us  [local(): received = lax.all_to_all(blocks, 'section', 1, 0)]
    while x30 -> x0, local copies, waits for them, and re-layouts: 21.9 us -> none
    ppermute x15 -> x0, starting transfers between devices: 19.2 us -> none  [passed_along(): return lax.ppermute(block, axis, route)]
  transfers between devices with their start and end apart: 16 -> 1, of which waited for: 16 -> 1; matrix products, arithmetic and copies ran while one was open for 0% -> 0% of each run, Pallas kernels for 0% -> 0%
where the time goes in v1:
time: 86 us; the launch traced here: 85.7 us
  blocking collectives  46.1 us (54%)
  waiting for transfers between devices  24.8 us (29%)
  starting transfers between devices  7.72 us (9%)
  local copies, waits for them, and re-layouts  3.73 us (4%)
  Pallas kernels  2.61 us (3%)
    all_to_all x2, blocking collectives, summed(): received = lax.all_to_all(block, axis, 0, 0)  46.1 us
    all_to_all x1, waiting for transfers between devices, local(): received = lax.all_to_all(blocks, 'section', 1, 0)  24.8 us
    all_to_all x1, starting transfers between devices, local(): received = lax.all_to_all(blocks, 'section', 1, 0)  7.72 us
    another operation x1, local copies, waits for them, and re-layouts, local(): received = lax.all_to_all(blocks, 'section', 1, 0)  3.07 us
    pallas_call x1, Pallas kernels, relay(): pl.pallas_call(relay_kernel, grid_spec=pltpu.PrefetchScalarGridSpec(num_s...  2.61 us
  transfers between devices with their start and end apart: 1, of which 1 were waited for; matrix products, arithmetic and copies ran while one was open for 0% of the time, Pallas kernels for 0%

profile of v1, /device:TPU:1, one launch (start us, length us, event | category | flops | bytes accessed | tf_op | source)
XLA Modules:
  0.0 85.7 jit_solution(5727063001228362264)
XLA Ops:
  0.6 3.1 %copy.7 = bf16[1,3,16,8,2688]{4,3,1,0,2:T(8,128)(2,1)} copy(bf16[1,3,16,8,2688]{4,3,2,1,0:T(8,128)(2,1)} %bitcast.14) | data formatting | bytes 4128768 | tf_op jit(solution)/shard_map/broadcast_in_dim;reshape;squeeze | solution.py:127
  3.7 0.0 copy-start
  3.7 0.0 copy-start.1
  3.7 0.0 copy-start.2
  3.7 7.7 %all-to-all-start = ((bf16[1,3,16,8,2688]{4,3,1,0,2:T(8,128)(2,1)}), bf16[1,3,16,8,2688]{4,3,1,0,2:T(8,128)(2,1)S(1)}, u32[]{:S(2)}, u32[]{:S(2)}) async-start(bf16[1,3,16,8,2688]{4,3,1,0,2:T(8,128)(2,1)} %copy.7), calls=%async_computation | async-start | bytes 4128768 | tf_op jit(solution)/shard_map/all_to_all | solution.py:127
  11.4 24.8 %all-to-all-done = bf16[1,3,16,8,2688]{4,3,1,0,2:T(8,128)(2,1)S(1)} async-done(((bf16[1,3,16,8,2688]{4,3,1,0,2:T(8,128)(2,1)}), bf16[1,3,16,8,2688]{4,3,1,0,2:T(8,128)(2,1)S(1)}, u32[]{:S(2)}, u32[]{:S(2)}) %all-to-all-start) | async-done | bytes 2064416 | tf_op jit(solution)/shard_map/all_to_all | solution.py:127
  36.3 0.0 copy-done
  36.3 0.0 copy-done.1
  36.3 0.0 copy-done.2
  36.3 2.6 %shard_map.59 = bf16[16,48,128]{2,1,0:T(8,128)(2,1)S(1)} custom-call(s32[1]{0:T(128)} %bitcast.position_ref, s32[16]{0:T(128)S(1)} %bitcast.13, bf16[48,8,2688]{2,1,0:T(8,128)(2,1)S(1)} %bitcast.11, bf16[16,8,2688]{2,1,0:T(8,128)(2,1)S(1)} %bitcast.12, f32[16,2688]{1,0:T(8,128)S(1)} %copy-done.1), custom_call_target="tpu_custom_call" | custom-call | flops 10321920 | bytes 1376256 | tf_op jit(solution)/shard_map/pallas_call | solution.py:88
  38.9 14.3 %all_to_all.25 = bf16[16,48,128]{2,1,0:T(8,128)(2,1)S(1)} all-to-all(bf16[16,48,128]{2,1,0:T(8,128)(2,1)S(1)} %shard_map.59), channel_id=1, replica_groups=mesh['replica'=32,'section'=16] {'section'}, dimensions={0} | all-to-all | bytes 393216 | tf_op jit(solution)/shard_map/all_to_all | solution.py:114
  53.3 0.1 reshape.11
  53.4 31.7 %all_to_all.26 = f32[32,2,84]{2,1,0:T(2,128)S(1)} all-to-all(f32[32,2,84]{2,1,0:T(2,128)S(1)} %copy.8), channel_id=1, replica_groups=mesh['replica'=32,'section'=16] {'replica'}, dimensions={0} | all-to-all | bytes 43008 | tf_op jit(solution)/shard_map/all_to_all | solution.py:114
  85.2 0.5 fusion
  (4 shorter events, 0.1 us)
Async XLA Ops:
  3.7 32.6 %copy-start = (bf16[1,128,2688]{2,1,0:T(8,128)(2,1)S(1)}, bf16[1,128,2688]{2,1,0:T(8,128)(2,1)}, u32[]{:S(2)}) copy-start(bf16[1,128,2688]{2,1,0:T(8,128)(2,1)} %param.5) | copy-start | bytes 2064388
  3.7 32.6 %copy-start.1 = (f32[16,2688]{1,0:T(8,128)S(1)}, f32[16,2688]{1,0:T(8,128)}, u32[]{:S(2)}) copy-start(f32[16,2688]{1,0:T(8,128)} %gains_ref.1) | copy-start | bytes 516100
  3.7 32.6 %copy-start.2 = (s32[1,16]{1,0:T(1,128)S(1)}, s32[1,16]{1,0:T(1,128)}, u32[]{:S(2)}) copy-start(s32[1,16]{1,0:T(1,128)} %param.7) | copy-start | bytes 196
  3.7 32.6 %all-to-all-start = ((bf16[1,3,16,8,2688]{4,3,1,0,2:T(8,128)(2,1)}), bf16[1,3,16,8,2688]{4,3,1,0,2:T(8,128)(2,1)S(1)}, u32[]{:S(2)}, u32[]{:S(2)}) async-start(bf16[1,3,16,8,2688]{4,3,1,0,2:T(8,128)(2,1)} %copy.7), calls=%async_computation | async-start | bytes 4128768 | tf_op jit(solution)/shard_map/all_to_all | solution.py:127

commit v2 on v1

--- a/solution.py
+++ b/solution.py
@@ -7,6 +7,33 @@
 
 epsilon = 1e-05
 lanes = 128
+
+
+def deal_kernel(saved_ref, out_ref, sems):
+    slot_count, sections = saved_ref.shape[:2]
+    parts = sems.shape[1]
+    copies = []
+    for slot in range(slot_count):
+        for part in range(parts):
+            at = pl.ds(part * (sections // parts), sections // parts)
+            copies.append(pltpu.make_async_copy(saved_ref.at[slot, at], out_ref.at[at, slot], sems.at[slot, part]))
+    for copy in copies:
+        copy.start()
+    for copy in copies:
+        copy.wait()
+
+
+def deal(saved):
+    slot_count, sections, rows, channels = saved.shape
+    return pl.pallas_call(
+        deal_kernel,
+        in_specs=[pl.BlockSpec(memory_space=pltpu.HBM)],
+        out_specs=pl.BlockSpec(memory_space=pltpu.VMEM),
+        scratch_shapes=[pltpu.SemaphoreType.DMA((slot_count, 4))],
+        out_shape=jax.ShapeDtypeStruct((sections, slot_count, rows, channels), saved.dtype),
+        compiler_params=pltpu.CompilerParams(vmem_limit_bytes=51 * 1024 * 1024),
+        cost_estimate=pl.CostEstimate(flops=1, bytes_accessed=1, transcendentals=0),
+    )(saved)
 
 
 def total(terms):
@@ -123,8 +150,8 @@
     replicas = lax.axis_size("replica")
     position = jnp.full((1,), lax.axis_index("section"), jnp.int32)
     rows = tokens // sections
-    blocks = saved.reshape(slot_count, sections, rows, channels)
-    received = lax.all_to_all(blocks, "section", 1, 0)
+    blocks = deal(saved.reshape(slot_count, sections, rows, channels))
+    received = lax.all_to_all(blocks, "section", 0, 0)
     slots = received.reshape(sections * slot_count, rows, channels)
     grad = grad_output[0].reshape(sections, rows, channels)
     partials = relay(position, layer_section[0], slots, grad, gains)

time: 86 us -> 86 us (level)
  local copies, waits for them, and re-layouts: 3.73 us -> 1.99 us
  Pallas kernels: 2.61 us -> 4.34 us
    another operation x1 -> x0, local copies, waits for them, and re-layouts: 3.07 us -> none  [local(): received = lax.all_to_all(blocks, 'section', 1, 0)]
    pallas_call x0 -> x1, Pallas kernels: none -> 1.73 us  [deal(): pl.pallas_call(deal_kernel, in_specs=[pl.BlockSpec(memory_space=pltpu.HBM...]
    unnamed x6 -> x8, local copies, waits for them, and re-layouts: 0.01 us -> 1.35 us
where the time goes in v2:
time: 86 us; the launch traced here: 85.7 us
  blocking collectives  46.1 us (54%)
  waiting for transfers between devices  24.8 us (29%)
  starting transfers between devices  7.72 us (9%)
  Pallas kernels  4.34 us (5%)
  local copies, waits for them, and re-layouts  1.99 us (2%)
    all_to_all x2, blocking collectives, summed(): received = lax.all_to_all(block, axis, 0, 0)  46.1 us
    all_to_all x1, waiting for transfers between devices, local(): received = lax.all_to_all(blocks, 'section', 0, 0)  24.8 us
    all_to_all x1, starting transfers between devices, local(): received = lax.all_to_all(blocks, 'section', 0, 0)  7.72 us
    pallas_call x1, Pallas kernels, relay(): pl.pallas_call(relay_kernel, grid_spec=pltpu.PrefetchScalarGridSpec(num_s...  2.61 us
    pallas_call x1, Pallas kernels, deal(): pl.pallas_call(deal_kernel, in_specs=[pl.BlockSpec(memory_space=pltpu.HBM...  1.73 us
  transfers between devices with their start and end apart: 1, of which 1 were waited for; matrix products, arithmetic and copies ran while one was open for 0% of the time, Pallas kernels for 0%

profile of v2, /device:TPU:1, one launch (start us, length us, event | category | flops | bytes accessed | tf_op | source)
XLA Modules:
  0.0 85.7 jit_solution(3673792002388079932)
XLA Ops:
  0.6 1.7 %shard_map.59 = bf16[16,3,8,2688]{3,2,1,0:T(8,128)(2,1)S(1)} custom-call(bf16[3,16,8,2688]{3,2,1,0:T(8,128)(2,1)} %bitcast.10), custom_call_target="tpu_custom_call" | custom-call | flops 1 | bytes 1 | tf_op jit(solution)/shard_map/pallas_call | solution.py:28
  2.4 0.0 copy-start
  2.4 1.3 %copy-done = bf16[16,3,8,2688]{3,2,1,0:T(8,128)(2,1)} copy-done((bf16[16,3,8,2688]{3,2,1,0:T(8,128)(2,1)}, bf16[16,3,8,2688]{3,2,1,0:T(8,128)(2,1)S(1)}, u32[]{:S(2)}) %copy-start) | copy-done | bytes 2064408
  3.7 0.0 copy-start.1
  3.7 0.0 copy-start.2
  3.7 0.0 copy-start.3
  3.7 7.7 %all-to-all-start = ((bf16[16,3,8,2688]{3,2,1,0:T(8,128)(2,1)}), bf16[16,3,8,2688]{3,2,1,0:T(8,128)(2,1)S(1)}, u32[]{:S(2)}, u32[]{:S(2)}) async-start(bf16[16,3,8,2688]{3,2,1,0:T(8,128)(2,1)} %copy-done), calls=%async_computation | async-start | bytes 4128768 | tf_op jit(solution)/shard_map/all_to_all | solution.py:154
  11.4 24.8 %all-to-all-done = bf16[16,3,8,2688]{3,2,1,0:T(8,128)(2,1)S(1)} async-done(((bf16[16,3,8,2688]{3,2,1,0:T(8,128)(2,1)}), bf16[16,3,8,2688]{3,2,1,0:T(8,128)(2,1)S(1)}, u32[]{:S(2)}, u32[]{:S(2)}) %all-to-all-start) | async-done | bytes 2064416 | tf_op jit(solution)/shard_map/all_to_all | solution.py:154
  36.3 0.0 copy-done.1
  36.3 0.0 copy-done.2
  36.3 0.0 copy-done.3
  36.3 2.6 %shard_map.60 = bf16[16,48,128]{2,1,0:T(8,128)(2,1)S(1)} custom-call(s32[1]{0:T(128)} %bitcast.position_ref, s32[16]{0:T(128)S(1)} %bitcast.9, bf16[48,8,2688]{2,1,0:T(8,128)(2,1)S(1)} %bitcast.7, bf16[16,8,2688]{2,1,0:T(8,128)(2,1)S(1)} %bitcast.8, f32[16,2688]{1,0:T(8,128)S(1)} %copy-done.2), custom_call_target="tpu_custom_call" | custom-call | flops 10321920 | bytes 1376256 | tf_op jit(solution)/shard_map/pallas_call | solution.py:115
  38.9 14.3 %all_to_all.15 = bf16[16,48,128]{2,1,0:T(8,128)(2,1)S(1)} all-to-all(bf16[16,48,128]{2,1,0:T(8,128)(2,1)S(1)} %shard_map.60), channel_id=1, replica_groups=mesh['replica'=32,'section'=16] {'section'}, dimensions={0} | all-to-all | bytes 393216 | tf_op jit(solution)/shard_map/all_to_all | solution.py:141
  53.3 0.1 reshape.14
  53.4 31.7 %all_to_all.16 = f32[32,2,84]{2,1,0:T(2,128)S(1)} all-to-all(f32[32,2,84]{2,1,0:T(2,128)S(1)} %copy.6), channel_id=1, replica_groups=mesh['replica'=32,'section'=16] {'replica'}, dimensions={0} | all-to-all | bytes 43008 | tf_op jit(solution)/shard_map/all_to_all | solution.py:141
  85.2 0.5 fusion
  (4 shorter events, 0.1 us)
Async XLA Ops:
  2.4 1.3 %copy-start = (bf16[16,3,8,2688]{3,2,1,0:T(8,128)(2,1)}, bf16[16,3,8,2688]{3,2,1,0:T(8,128)(2,1)S(1)}, u32[]{:S(2)}) copy-start(bf16[16,3,8,2688]{3,2,1,0:T(8,128)(2,1)S(1)} %shard_map.59) | copy-start | bytes 6193156
  3.7 32.6 %copy-start.1 = (bf16[1,128,2688]{2,1,0:T(8,128)(2,1)S(1)}, bf16[1,128,2688]{2,1,0:T(8,128)(2,1)}, u32[]{:S(2)}) copy-start(bf16[1,128,2688]{2,1,0:T(8,128)(2,1)} %param.5) | copy-start | bytes 2064388
  3.7 32.6 %copy-start.2 = (f32[16,2688]{1,0:T(8,128)S(1)}, f32[16,2688]{1,0:T(8,128)}, u32[]{:S(2)}) copy-start(f32[16,2688]{1,0:T(8,128)} %gains_ref.1) | copy-start | bytes 516100
  3.7 32.6 %copy-start.3 = (s32[1,16]{1,0:T(1,128)S(1)}, s32[1,16]{1,0:T(1,128)}, u32[]{:S(2)}) copy-start(s32[1,16]{1,0:T(1,128)} %param.7) | copy-start | bytes 196
  3.7 32.6 %all-to-all-start = ((bf16[16,3,8,2688]{3,2,1,0:T(8,128)(2,1)}), bf16[16,3,8,2688]{3,2,1,0:T(8,128)(2,1)S(1)}, u32[]{:S(2)}, u32[]{:S(2)}) async-start(bf16[16,3,8,2688]{3,2,1,0:T(8,128)(2,1)} %copy-done), calls=%async_computation | async-start | bytes 4128768 | tf_op jit(solution)/shard_map/all_to_all | solution.py:154

commit v3 on v2

--- a/solution.py
+++ b/solution.py
@@ -9,18 +9,24 @@
 lanes = 128
 
 
-def deal_kernel(saved_ref, out_ref, sems):
+def deal_kernel(saved_ref, out_ref, held_ref, in_sems, out_sems):
     slot_count, sections = saved_ref.shape[:2]
-    parts = sems.shape[1]
-    copies = []
-    for slot in range(slot_count):
-        for part in range(parts):
-            at = pl.ds(part * (sections // parts), sections // parts)
-            copies.append(pltpu.make_async_copy(saved_ref.at[slot, at], out_ref.at[at, slot], sems.at[slot, part]))
-    for copy in copies:
+    parts = in_sems.shape[1]
+    step = sections // parts
+    inward, outward = [], []
+    for part in range(parts):
+        for slot in range(slot_count):
+            at = pl.ds(part * step, step)
+            held = held_ref.at[slot, at]
+            inward.append(pltpu.make_async_copy(saved_ref.at[slot, at], held, in_sems.at[slot, part]))
+            outward.append(pltpu.make_async_copy(held, out_ref.at[at, slot], out_sems.at[slot, part]))
+    for copy in inward:
         copy.start()
-    for copy in copies:
+    for copy, onward in zip(inward, outward):
         copy.wait()
+        onward.start()
+    for onward in outward:
+        onward.wait()
 
 
 def deal(saved):
@@ -28,10 +34,14 @@
     return pl.pallas_call(
         deal_kernel,
         in_specs=[pl.BlockSpec(memory_space=pltpu.HBM)],
-        out_specs=pl.BlockSpec(memory_space=pltpu.VMEM),
-        scratch_shapes=[pltpu.SemaphoreType.DMA((slot_count, 4))],
+        out_specs=pl.BlockSpec(memory_space=pltpu.HBM),
+        scratch_shapes=[
+            pltpu.VMEM(saved.shape, saved.dtype),
+            pltpu.SemaphoreType.DMA((slot_count, 8)),
+            pltpu.SemaphoreType.DMA((slot_count, 8)),
+        ],
         out_shape=jax.ShapeDtypeStruct((sections, slot_count, rows, channels), saved.dtype),
-        compiler_params=pltpu.CompilerParams(vmem_limit_bytes=51 * 1024 * 1024),
+        compiler_params=pltpu.CompilerParams(vmem_limit_bytes=56 * 1024 * 1024),
         cost_estimate=pl.CostEstimate(flops=1, bytes_accessed=1, transcendentals=0),
     )(saved)
 

time: 86 us -> 85.8 us (level)
  local copies, waits for them, and re-layouts: 1.99 us -> 0.67 us
  Pallas kernels: 4.34 us -> 5.39 us
    unnamed x8 -> x6, local copies, waits for them, and re-layouts: 1.35 us -> 0.02 us
    pallas_call x1, Pallas kernels: 1.73 us -> 2.78 us  [deal(): pl.pallas_call(deal_kernel, in_specs=[pl.BlockSpec(memory_space=pltpu.HBM...]
where the time goes in v3:
time: 85.8 us; the launch traced here: 85.5 us
  blocking collectives  46.1 us (54%)
  waiting for transfers between devices  24.8 us (29%)
  starting transfers between devices  7.73 us (9%)
  Pallas kernels  5.39 us (6%)
    all_to_all x2, blocking collectives, summed(): received = lax.all_to_all(block, axis, 0, 0)  46.1 us
    all_to_all x1, waiting for transfers between devices, local(): received = lax.all_to_all(blocks, 'section', 0, 0)  24.8 us
    all_to_all x1, starting transfers between devices, local(): received = lax.all_to_all(blocks, 'section', 0, 0)  7.73 us
    pallas_call x1, Pallas kernels, deal(): pl.pallas_call(deal_kernel, in_specs=[pl.BlockSpec(memory_space=pltpu.HBM...  2.78 us
    pallas_call x1, Pallas kernels, relay(): pl.pallas_call(relay_kernel, grid_spec=pltpu.PrefetchScalarGridSpec(num_s...  2.61 us
  transfers between devices with their start and end apart: 1, of which 1 were waited for; matrix products, arithmetic and copies ran while one was open for 0% of the time, Pallas kernels for 0%

profile of v3, /device:TPU:1, one launch (start us, length us, event | category | flops | bytes accessed | tf_op | source)
XLA Modules:
  0.0 85.5 jit_solution(11581462045348915829)
XLA Ops:
  0.6 2.8 %shard_map.59 = bf16[16,3,8,2688]{3,2,1,0:T(8,128)(2,1)} custom-call(bf16[3,16,8,2688]{3,2,1,0:T(8,128)(2,1)} %bitcast.10), custom_call_target="tpu_custom_call" | custom-call | flops 1 | bytes 1 | tf_op jit(solution)/shard_map/pallas_call | solution.py:34
  3.4 0.0 copy-start
  3.4 0.0 copy-start.1
  3.4 0.0 copy-start.2
  3.4 7.7 %all-to-all-start = ((bf16[16,3,8,2688]{3,2,1,0:T(8,128)(2,1)}), bf16[16,3,8,2688]{3,2,1,0:T(8,128)(2,1)S(1)}, u32[]{:S(2)}, u32[]{:S(2)}) async-start(bf16[16,3,8,2688]{3,2,1,0:T(8,128)(2,1)} %shard_map.59), calls=%async_computation | async-start | bytes 4128768 | tf_op jit(solution)/shard_map/all_to_all | solution.py:164
  11.2 24.8 %all-to-all-done = bf16[16,3,8,2688]{3,2,1,0:T(8,128)(2,1)S(1)} async-done(((bf16[16,3,8,2688]{3,2,1,0:T(8,128)(2,1)}), bf16[16,3,8,2688]{3,2,1,0:T(8,128)(2,1)S(1)}, u32[]{:S(2)}, u32[]{:S(2)}) %all-to-all-start) | async-done | bytes 2064416 | tf_op jit(solution)/shard_map/all_to_all | solution.py:164
  36.0 0.0 copy-done
  36.0 0.0 copy-done.1
  36.0 0.0 copy-done.2
  36.0 2.6 %shard_map.60 = bf16[16,48,128]{2,1,0:T(8,128)(2,1)S(1)} custom-call(s32[1]{0:T(128)} %bitcast.position_ref, s32[16]{0:T(128)S(1)} %bitcast.9, bf16[48,8,2688]{2,1,0:T(8,128)(2,1)S(1)} %bitcast.7, bf16[16,8,2688]{2,1,0:T(8,128)(2,1)S(1)} %bitcast.8, f32[16,2688]{1,0:T(8,128)S(1)} %copy-done.1), custom_call_target="tpu_custom_call" | custom-call | flops 10321920 | bytes 1376256 | tf_op jit(solution)/shard_map/pallas_call | solution.py:125
  38.7 14.3 %all_to_all.15 = bf16[16,48,128]{2,1,0:T(8,128)(2,1)S(1)} all-to-all(bf16[16,48,128]{2,1,0:T(8,128)(2,1)S(1)} %shard_map.60), channel_id=1, replica_groups=mesh['replica'=32,'section'=16] {'section'}, dimensions={0} | all-to-all | bytes 393216 | tf_op jit(solution)/shard_map/all_to_all | solution.py:151
  53.0 0.1 reshape.14
  53.2 31.7 %all_to_all.16 = f32[32,2,84]{2,1,0:T(2,128)S(1)} all-to-all(f32[32,2,84]{2,1,0:T(2,128)S(1)} %copy.6), channel_id=1, replica_groups=mesh['replica'=32,'section'=16] {'replica'}, dimensions={0} | all-to-all | bytes 43008 | tf_op jit(solution)/shard_map/all_to_all | solution.py:151
  85.0 0.5 fusion
  (4 shorter events, 0.1 us)
Async XLA Ops:
  3.4 32.6 %copy-start = (bf16[1,128,2688]{2,1,0:T(8,128)(2,1)S(1)}, bf16[1,128,2688]{2,1,0:T(8,128)(2,1)}, u32[]{:S(2)}) copy-start(bf16[1,128,2688]{2,1,0:T(8,128)(2,1)} %param.5) | copy-start | bytes 2064388
  3.4 32.6 %copy-start.1 = (f32[16,2688]{1,0:T(8,128)S(1)}, f32[16,2688]{1,0:T(8,128)}, u32[]{:S(2)}) copy-start(f32[16,2688]{1,0:T(8,128)} %gains_ref.1) | copy-start | bytes 516100
  3.4 32.6 %copy-start.2 = (s32[1,16]{1,0:T(1,128)S(1)}, s32[1,16]{1,0:T(1,128)}, u32[]{:S(2)}) copy-start(s32[1,16]{1,0:T(1,128)} %param.7) | copy-start | bytes 196
  3.4 32.6 %all-to-all-start = ((bf16[16,3,8,2688]{3,2,1,0:T(8,128)(2,1)}), bf16[16,3,8,2688]{3,2,1,0:T(8,128)(2,1)S(1)}, u32[]{:S(2)}, u32[]{:S(2)}) async-start(bf16[16,3,8,2688]{3,2,1,0:T(8,128)(2,1)} %shard_map.59), calls=%async_computation | async-start | bytes 4128768 | tf_op jit(solution)/shard_map/all_to_all | solution.py:164

commit v4 on v3

--- a/solution.py
+++ b/solution.py
@@ -113,7 +113,7 @@
             packed = jnp.concatenate([fold(sums[at:at + 8]), fold(sums[at + 8:at + 16])], axis=0)
             out_ref[row, at:at + 16] = packed.astype(out_ref.dtype)
         gradient = [
-            (g + inverse[layer] * u) - (along_one + along_normed * n)
+            ((g + inverse[layer] * u) - (along_one + along_normed * n)).astype(jnp.bfloat16).astype(jnp.float32)
             for g, u, n in zip(gradient, scaled, normed)
         ]
 

time: 85.8 us -> 85.9 us (level)
  no operation moved by 1% of the time
where the time goes in v4:
time: 85.9 us; the launch traced here: 85.6 us
  blocking collectives  46.1 us (54%)
  waiting for transfers between devices  24.8 us (29%)
  starting transfers between devices  7.73 us (9%)
  Pallas kernels  5.47 us (6%)
    all_to_all x2, blocking collectives, summed(): received = lax.all_to_all(block, axis, 0, 0)  46.1 us
    all_to_all x1, waiting for transfers between devices, local(): received = lax.all_to_all(blocks, 'section', 0, 0)  24.8 us
    all_to_all x1, starting transfers between devices, local(): received = lax.all_to_all(blocks, 'section', 0, 0)  7.73 us
    pallas_call x1, Pallas kernels, deal(): pl.pallas_call(deal_kernel, in_specs=[pl.BlockSpec(memory_space=pltpu.HBM...  2.78 us
    pallas_call x1, Pallas kernels, relay(): pl.pallas_call(relay_kernel, grid_spec=pltpu.PrefetchScalarGridSpec(num_s...  2.69 us
  transfers between devices with their start and end apart: 1, of which 1 were waited for; matrix products, arithmetic and copies ran while one was open for 0% of the time, Pallas kernels for 0%

profile of v4, /device:TPU:1, one launch (start us, length us, event | category | flops | bytes accessed | tf_op | source)
XLA Modules:
  0.0 85.6 jit_solution(10142952676419266630)
XLA Ops:
  0.6 2.8 %shard_map.59 = bf16[16,3,8,2688]{3,2,1,0:T(8,128)(2,1)} custom-call(bf16[3,16,8,2688]{3,2,1,0:T(8,128)(2,1)} %bitcast.10), custom_call_target="tpu_custom_call" | custom-call | flops 1 | bytes 1 | tf_op jit(solution)/shard_map/pallas_call | solution.py:34
  3.4 0.0 copy-start
  3.4 0.0 copy-start.1
  3.4 0.0 copy-start.2
  3.4 7.7 %all-to-all-start = ((bf16[16,3,8,2688]{3,2,1,0:T(8,128)(2,1)}), bf16[16,3,8,2688]{3,2,1,0:T(8,128)(2,1)S(1)}, u32[]{:S(2)}, u32[]{:S(2)}) async-start(bf16[16,3,8,2688]{3,2,1,0:T(8,128)(2,1)} %shard_map.59), calls=%async_computation | async-start | bytes 4128768 | tf_op jit(solution)/shard_map/all_to_all | solution.py:164
  11.2 24.8 %all-to-all-done = bf16[16,3,8,2688]{3,2,1,0:T(8,128)(2,1)S(1)} async-done(((bf16[16,3,8,2688]{3,2,1,0:T(8,128)(2,1)}), bf16[16,3,8,2688]{3,2,1,0:T(8,128)(2,1)S(1)}, u32[]{:S(2)}, u32[]{:S(2)}) %all-to-all-start) | async-done | bytes 2064416 | tf_op jit(solution)/shard_map/all_to_all | solution.py:164
  36.0 0.0 copy-done
  36.0 0.0 copy-done.1
  36.0 0.0 copy-done.2
  36.0 2.7 %shard_map.60 = bf16[16,48,128]{2,1,0:T(8,128)(2,1)S(1)} custom-call(s32[1]{0:T(128)} %bitcast.position_ref, s32[16]{0:T(128)S(1)} %bitcast.9, bf16[48,8,2688]{2,1,0:T(8,128)(2,1)S(1)} %bitcast.7, bf16[16,8,2688]{2,1,0:T(8,128)(2,1)S(1)} %bitcast.8, f32[16,2688]{1,0:T(8,128)S(1)} %copy-done.1), custom_call_target="tpu_custom_call" | custom-call | flops 10321920 | bytes 1376256 | tf_op jit(solution)/shard_map/pallas_call | solution.py:125
  38.7 14.3 %all_to_all.15 = bf16[16,48,128]{2,1,0:T(8,128)(2,1)S(1)} all-to-all(bf16[16,48,128]{2,1,0:T(8,128)(2,1)S(1)} %shard_map.60), channel_id=1, replica_groups=mesh['replica'=32,'section'=16] {'section'}, dimensions={0} | all-to-all | bytes 393216 | tf_op jit(solution)/shard_map/all_to_all | solution.py:151
  53.1 0.1 reshape.14
  53.3 31.7 %all_to_all.16 = f32[32,2,84]{2,1,0:T(2,128)S(1)} all-to-all(f32[32,2,84]{2,1,0:T(2,128)S(1)} %copy.6), channel_id=1, replica_groups=mesh['replica'=32,'section'=16] {'replica'}, dimensions={0} | all-to-all | bytes 43008 | tf_op jit(solution)/shard_map/all_to_all | solution.py:151
  85.0 0.5 fusion
  (4 shorter events, 0.1 us)
Async XLA Ops:
  3.4 32.6 %copy-start = (bf16[1,128,2688]{2,1,0:T(8,128)(2,1)S(1)}, bf16[1,128,2688]{2,1,0:T(8,128)(2,1)}, u32[]{:S(2)}) copy-start(bf16[1,128,2688]{2,1,0:T(8,128)(2,1)} %param.5) | copy-start | bytes 2064388
  3.4 32.6 %copy-start.1 = (f32[16,2688]{1,0:T(8,128)S(1)}, f32[16,2688]{1,0:T(8,128)}, u32[]{:S(2)}) copy-start(f32[16,2688]{1,0:T(8,128)} %gains_ref.1) | copy-start | bytes 516100
  3.4 32.6 %copy-start.2 = (s32[1,16]{1,0:T(1,128)S(1)}, s32[1,16]{1,0:T(1,128)}, u32[]{:S(2)}) copy-start(s32[1,16]{1,0:T(1,128)} %param.7) | copy-start | bytes 196
  3.4 32.6 %all-to-all-start = ((bf16[16,3,8,2688]{3,2,1,0:T(8,128)(2,1)}), bf16[16,3,8,2688]{3,2,1,0:T(8,128)(2,1)S(1)}, u32[]{:S(2)}, u32[]{:S(2)}) async-start(bf16[16,3,8,2688]{3,2,1,0:T(8,128)(2,1)} %shard_map.59), calls=%async_computation | async-start | bytes 4128768 | tf_op jit(solution)/shard_map/all_to_all | solution.py:164

commit v5 on v4

--- a/solution.py
+++ b/solution.py
@@ -20,11 +20,14 @@
             held = held_ref.at[slot, at]
             inward.append(pltpu.make_async_copy(saved_ref.at[slot, at], held, in_sems.at[slot, part]))
             outward.append(pltpu.make_async_copy(held, out_ref.at[at, slot], out_sems.at[slot, part]))
-    for copy in inward:
+    ahead = 6
+    for copy in inward[:ahead]:
         copy.start()
-    for copy, onward in zip(inward, outward):
+    for index, (copy, onward) in enumerate(zip(inward, outward)):
         copy.wait()
         onward.start()
+        if index + ahead < len(inward):
+            inward[index + ahead].start()
     for onward in outward:
         onward.wait()
 
@@ -71,8 +74,8 @@
     return jnp.where(index % 2 < 1, a + pltpu.roll(a, 7, 0), b + pltpu.roll(b, 1, 0))
 
 
-def relay_kernel(position_ref, map_ref, slots_ref, grad_ref, gains_ref, out_ref, held_ref, normed_ref, sem):
-    layers, rows, channels = normed_ref.shape
+def relay_kernel(position_ref, map_ref, slots_ref, grad_ref, gains_ref, out_ref, held_ref, centered_ref, sem):
+    layers, rows, channels = centered_ref.shape
     slot_count = slots_ref.shape[0] // out_ref.shape[0]
     columns = [slice(at, at + lanes) for at in range(0, channels, lanes)]
     share = 1.0 / channels
@@ -92,20 +95,20 @@
     inverse = {}
     for layer in order:
         centered = [tile - average[layer] for tile in tiles(layer)]
+        for at, tile in zip(columns, centered):
+            centered_ref[layer, :, at] = tile
         inverse[layer] = lax.rsqrt(across(total([tile * tile for tile in centered])) * share + epsilon)
-    for layer in order:
-        for at, tile in zip(columns, tiles(layer)):
-            normed_ref[layer, :, at] = (tile - average[layer]) * inverse[layer]
     fetch.wait()
     gradient = [held_ref[:, at].astype(jnp.float32) for at in columns]
     blank = jnp.zeros((rows, lanes), jnp.float32)
     for layer in order:
-        normed = [normed_ref[layer, :, at] for at in columns]
+        normed = [centered_ref[layer, :, at] * inverse[layer] for at in columns]
+        weight = inverse[layer] * share
         along = [g * n for g, n in zip(gradient, normed)]
         gain = [gains_ref[layer:layer + 1, at] for at in columns]
         scaled = [g * c for g, c in zip(gradient, gain)]
-        along_one = across(total(scaled)) * share * inverse[layer]
-        along_normed = across(total([p * c for p, c in zip(along, gain)])) * share * inverse[layer]
+        along_one = across(total(scaled)) * weight
+        along_normed = across(total([p * c for p, c in zip(along, gain)])) * weight
         sums = along + gradient
         sums = sums + [blank] * (-len(sums) % 16)
         row = layers - 1 - layer

time: 85.9 us -> 88.7 us (1.033)
  Pallas kernels: 5.47 us -> 8.12 us
    pallas_call x1, Pallas kernels: 2.78 us -> 5.38 us  [deal(): pl.pallas_call(deal_kernel, in_specs=[pl.BlockSpec(memory_space=pltpu.HBM...]
where the time goes in v5:
time: 88.7 us; the launch traced here: 88.2 us
  blocking collectives  46.1 us (52%)
  waiting for transfers between devices  24.8 us (28%)
  Pallas kernels  8.12 us (9%)
  starting transfers between devices  7.73 us (9%)
    all_to_all x2, blocking collectives, summed(): received = lax.all_to_all(block, axis, 0, 0)  46.1 us
    all_to_all x1, waiting for transfers between devices, local(): received = lax.all_to_all(blocks, 'section', 0, 0)  24.8 us
    all_to_all x1, starting transfers between devices, local(): received = lax.all_to_all(blocks, 'section', 0, 0)  7.73 us
    pallas_call x1, Pallas kernels, deal(): pl.pallas_call(deal_kernel, in_specs=[pl.BlockSpec(memory_space=pltpu.HBM...  5.38 us
    pallas_call x1, Pallas kernels, relay(): pl.pallas_call(relay_kernel, grid_spec=pltpu.PrefetchScalarGridSpec(num_s...  2.73 us
  transfers between devices with their start and end apart: 1, of which 1 were waited for; matrix products, arithmetic and copies ran while one was open for 0% of the time, Pallas kernels for 0%

profile of v5, /device:TPU:1, one launch (start us, length us, event | category | flops | bytes accessed | tf_op | source)
XLA Modules:
  0.0 88.2 jit_solution(3375060021857218501)
XLA Ops:
  0.6 5.4 %shard_map.59 = bf16[16,3,8,2688]{3,2,1,0:T(8,128)(2,1)} custom-call(bf16[3,16,8,2688]{3,2,1,0:T(8,128)(2,1)} %bitcast.10), custom_call_target="tpu_custom_call" | custom-call | flops 1 | bytes 1 | tf_op jit(solution)/shard_map/pallas_call | solution.py:37
  6.0 0.0 copy-start
  6.0 0.0 copy-start.1
  6.0 0.0 copy-start.2
  6.1 7.7 %all-to-all-start = ((bf16[16,3,8,2688]{3,2,1,0:T(8,128)(2,1)}), bf16[16,3,8,2688]{3,2,1,0:T(8,128)(2,1)S(1)}, u32[]{:S(2)}, u32[]{:S(2)}) async-start(bf16[16,3,8,2688]{3,2,1,0:T(8,128)(2,1)} %shard_map.59), calls=%async_computation | async-start | bytes 4128768 | tf_op jit(solution)/shard_map/all_to_all | solution.py:167
  13.8 24.8 %all-to-all-done = bf16[16,3,8,2688]{3,2,1,0:T(8,128)(2,1)S(1)} async-done(((bf16[16,3,8,2688]{3,2,1,0:T(8,128)(2,1)}), bf16[16,3,8,2688]{3,2,1,0:T(8,128)(2,1)S(1)}, u32[]{:S(2)}, u32[]{:S(2)}) %all-to-all-start) | async-done | bytes 2064416 | tf_op jit(solution)/shard_map/all_to_all | solution.py:167
  38.6 0.0 copy-done
  38.6 0.0 copy-done.1
  38.6 0.0 copy-done.2
  38.6 2.7 %shard_map.60 = bf16[16,48,128]{2,1,0:T(8,128)(2,1)S(1)} custom-call(s32[1]{0:T(128)} %bitcast.position_ref, s32[16]{0:T(128)S(1)} %bitcast.9, bf16[48,8,2688]{2,1,0:T(8,128)(2,1)S(1)} %bitcast.7, bf16[16,8,2688]{2,1,0:T(8,128)(2,1)S(1)} %bitcast.8, f32[16,2688]{1,0:T(8,128)S(1)} %copy-done.1), custom_call_target="tpu_custom_call" | custom-call | flops 10321920 | bytes 1376256 | tf_op jit(solution)/shard_map/pallas_call | solution.py:128
  41.4 14.4 %all_to_all.15 = bf16[16,48,128]{2,1,0:T(8,128)(2,1)S(1)} all-to-all(bf16[16,48,128]{2,1,0:T(8,128)(2,1)S(1)} %shard_map.60), channel_id=1, replica_groups=mesh['replica'=32,'section'=16] {'section'}, dimensions={0} | all-to-all | bytes 393216 | tf_op jit(solution)/shard_map/all_to_all | solution.py:154
  55.8 0.1 reshape.14
  55.9 31.7 %all_to_all.16 = f32[32,2,84]{2,1,0:T(2,128)S(1)} all-to-all(f32[32,2,84]{2,1,0:T(2,128)S(1)} %copy.6), channel_id=1, replica_groups=mesh['replica'=32,'section'=16] {'replica'}, dimensions={0} | all-to-all | bytes 43008 | tf_op jit(solution)/shard_map/all_to_all | solution.py:154
  87.7 0.5 fusion
  (4 shorter events, 0.1 us)
Async XLA Ops:
  6.0 32.6 %copy-start = (bf16[1,128,2688]{2,1,0:T(8,128)(2,1)S(1)}, bf16[1,128,2688]{2,1,0:T(8,128)(2,1)}, u32[]{:S(2)}) copy-start(bf16[1,128,2688]{2,1,0:T(8,128)(2,1)} %param.5) | copy-start | bytes 2064388
  6.0 32.6 %copy-start.1 = (f32[16,2688]{1,0:T(8,128)S(1)}, f32[16,2688]{1,0:T(8,128)}, u32[]{:S(2)}) copy-start(f32[16,2688]{1,0:T(8,128)} %gains_ref.1) | copy-start | bytes 516100
  6.0 32.6 %copy-start.2 = (s32[1,16]{1,0:T(1,128)S(1)}, s32[1,16]{1,0:T(1,128)}, u32[]{:S(2)}) copy-start(s32[1,16]{1,0:T(1,128)} %param.7) | copy-start | bytes 196
  6.1 32.6 %all-to-all-start = ((bf16[16,3,8,2688]{3,2,1,0:T(8,128)(2,1)}), bf16[16,3,8,2688]{3,2,1,0:T(8,128)(2,1)S(1)}, u32[]{:S(2)}, u32[]{:S(2)}) async-start(bf16[16,3,8,2688]{3,2,1,0:T(8,128)(2,1)} %shard_map.59), calls=%async_computation | async-start | bytes 4128768 | tf_op jit(solution)/shard_map/all_to_all | solution.py:167

commit v6 on v4

--- a/solution.py
+++ b/solution.py
@@ -24,7 +24,7 @@
         copy.start()
     for copy, onward in zip(inward, outward):
         copy.wait()
-        onward.start()
+        onward.start(priority=1)
     for onward in outward:
         onward.wait()
 

time: 85.9 us -> 85.9 us (level)
  no operation moved by 1% of the time
where the time goes in v6:
time: 85.9 us; the launch traced here: 85.6 us
  blocking collectives  46.1 us (54%)
  waiting for transfers between devices  24.8 us (29%)
  starting transfers between devices  7.73 us (9%)
  Pallas kernels  5.47 us (6%)
    all_to_all x2, blocking collectives, summed(): received = lax.all_to_all(block, axis, 0, 0)  46.1 us
    all_to_all x1, waiting for transfers between devices, local(): received = lax.all_to_all(blocks, 'section', 0, 0)  24.8 us
    all_to_all x1, starting transfers between devices, local(): received = lax.all_to_all(blocks, 'section', 0, 0)  7.73 us
    pallas_call x1, Pallas kernels, deal(): pl.pallas_call(deal_kernel, in_specs=[pl.BlockSpec(memory_space=pltpu.HBM...  2.78 us
    pallas_call x1, Pallas kernels, relay(): pl.pallas_call(relay_kernel, grid_spec=pltpu.PrefetchScalarGridSpec(num_s...  2.69 us
  transfers between devices with their start and end apart: 1, of which 1 were waited for; matrix products, arithmetic and copies ran while one was open for 0% of the time, Pallas kernels for 0%

profile of v6, /device:TPU:1, one launch (start us, length us, event | category | flops | bytes accessed | tf_op | source)
XLA Modules:
  0.0 85.6 jit_solution(10681102146224816474)
XLA Ops:
  0.6 2.8 %shard_map.59 = bf16[16,3,8,2688]{3,2,1,0:T(8,128)(2,1)} custom-call(bf16[3,16,8,2688]{3,2,1,0:T(8,128)(2,1)} %bitcast.10), custom_call_target="tpu_custom_call" | custom-call | flops 1 | bytes 1 | tf_op jit(solution)/shard_map/pallas_call | solution.py:34
  3.4 0.0 copy-start
  3.4 0.0 copy-start.1
  3.4 0.0 copy-start.2
  3.4 7.7 %all-to-all-start = ((bf16[16,3,8,2688]{3,2,1,0:T(8,128)(2,1)}), bf16[16,3,8,2688]{3,2,1,0:T(8,128)(2,1)S(1)}, u32[]{:S(2)}, u32[]{:S(2)}) async-start(bf16[16,3,8,2688]{3,2,1,0:T(8,128)(2,1)} %shard_map.59), calls=%async_computation | async-start | bytes 4128768 | tf_op jit(solution)/shard_map/all_to_all | solution.py:164
  11.2 24.8 %all-to-all-done = bf16[16,3,8,2688]{3,2,1,0:T(8,128)(2,1)S(1)} async-done(((bf16[16,3,8,2688]{3,2,1,0:T(8,128)(2,1)}), bf16[16,3,8,2688]{3,2,1,0:T(8,128)(2,1)S(1)}, u32[]{:S(2)}, u32[]{:S(2)}) %all-to-all-start) | async-done | bytes 2064416 | tf_op jit(solution)/shard_map/all_to_all | solution.py:164
  36.0 0.0 copy-done
  36.0 0.0 copy-done.1
  36.0 0.0 copy-done.2
  36.0 2.7 %shard_map.60 = bf16[16,48,128]{2,1,0:T(8,128)(2,1)S(1)} custom-call(s32[1]{0:T(128)} %bitcast.position_ref, s32[16]{0:T(128)S(1)} %bitcast.9, bf16[48,8,2688]{2,1,0:T(8,128)(2,1)S(1)} %bitcast.7, bf16[16,8,2688]{2,1,0:T(8,128)(2,1)S(1)} %bitcast.8, f32[16,2688]{1,0:T(8,128)S(1)} %copy-done.1), custom_call_target="tpu_custom_call" | custom-call | flops 10321920 | bytes 1376256 | tf_op jit(solution)/shard_map/pallas_call | solution.py:125
  38.7 14.3 %all_to_all.15 = bf16[16,48,128]{2,1,0:T(8,128)(2,1)S(1)} all-to-all(bf16[16,48,128]{2,1,0:T(8,128)(2,1)S(1)} %shard_map.60), channel_id=1, replica_groups=mesh['replica'=32,'section'=16] {'section'}, dimensions={0} | all-to-all | bytes 393216 | tf_op jit(solution)/shard_map/all_to_all | solution.py:151
  53.1 0.1 reshape.14
  53.3 31.7 %all_to_all.16 = f32[32,2,84]{2,1,0:T(2,128)S(1)} all-to-all(f32[32,2,84]{2,1,0:T(2,128)S(1)} %copy.6), channel_id=1, replica_groups=mesh['replica'=32,'section'=16] {'replica'}, dimensions={0} | all-to-all | bytes 43008 | tf_op jit(solution)/shard_map/all_to_all | solution.py:151
  85.0 0.5 fusion
  (4 shorter events, 0.1 us)
Async XLA Ops:
  3.4 32.6 %copy-start = (bf16[1,128,2688]{2,1,0:T(8,128)(2,1)S(1)}, bf16[1,128,2688]{2,1,0:T(8,128)(2,1)}, u32[]{:S(2)}) copy-start(bf16[1,128,2688]{2,1,0:T(8,128)(2,1)} %param.5) | copy-start | bytes 2064388
  3.4 32.6 %copy-start.1 = (f32[16,2688]{1,0:T(8,128)S(1)}, f32[16,2688]{1,0:T(8,128)}, u32[]{:S(2)}) copy-start(f32[16,2688]{1,0:T(8,128)} %gains_ref.1) | copy-start | bytes 516100
  3.4 32.6 %copy-start.2 = (s32[1,16]{1,0:T(1,128)S(1)}, s32[1,16]{1,0:T(1,128)}, u32[]{:S(2)}) copy-start(s32[1,16]{1,0:T(1,128)} %param.7) | copy-start | bytes 196
  3.4 32.6 %all-to-all-start = ((bf16[16,3,8,2688]{3,2,1,0:T(8,128)(2,1)}), bf16[16,3,8,2688]{3,2,1,0:T(8,128)(2,1)S(1)}, u32[]{:S(2)}, u32[]{:S(2)}) async-start(bf16[16,3,8,2688]{3,2,1,0:T(8,128)(2,1)} %shard_map.59), calls=%async_computation | async-start | bytes 4128768 | tf_op jit(solution)/shard_map/all_to_all | solution.py:164
